TPU v7x, 1024 devices: a whole 4x8x16 slice. The times are simulated.
1024 devices in a mesh: dp: 8 (over z_hi, x), expert: 8 (over y), etp: 16 (over z_lo, core).
Axes of the slice: x: 4, y: 8, z: 16 (z_hi: 2, z_lo: 8; z = z_hi * 8 + z_lo), core: 2. Of those that a mesh axis runs over, the one named last changes fastest.
Arguments:
- grad_out: bfloat16 [4096, 6144], P(('dp', 'expert'), 'etp'), may hold values from -1.5 to 1.5
- routes: int32 [4096, 2], P(('dp', 'expert')), may hold values from 0 to 7, all different within a row; in each aligned block of 64 rows (0 to 63, 64 to 127, ...) at most 32 rows name the same one
- gate_weights: bfloat16 [4096, 2], P(('dp', 'expert')), may hold values from 0.099609375 to 1
- saved_hidden: bfloat16 [8, 8, 2, 256, 8192], P('dp', 'expert', None, None, 'etp'), may hold values from -6 to 6
- down_weight: bfloat16 [8, 8192, 6144], P('expert', 'etp'), may hold values from -0.0625 to 0.0625
Outputs:
- hidden_grad: bfloat16 [8, 8, 2, 256, 8192], P('dp', 'expert', None, None, 'etp')
- weight_grad: bfloat16 [8, 6144, 8192], P('expert', 'dp', 'etp')
Inputs may be any that keep to these rules, and one draw needn't show every extreme that they name: `routes`: the two experts of a token differ; within each aligned block of 64 rows (one group) each expert is named at most 32 times.
All inputs are finite; a program needn't handle non-finite values.
Results may differ from a plain program's by a relative error of at most 0.0049.
Values may be sent and summed in bfloat16 or wider, within the bound.
A program may use at most 64 MiB of HBM per device.

v0:
```python
import jax
import jax.numpy as jnp
from jax import lax
from jax.sharding import PartitionSpec as P


def contract_first(left, right):
    return lax.dot_general(
        left, right, (((0,), (0,)), ((), ())), preferred_element_type=jnp.float32
    )


def contract_last(left, right):
    return lax.dot_general(
        left, right, (((1,), (1,)), ((), ())), preferred_element_type=jnp.float32
    )


def per_device(grad_out, routes, gate_weights, saved_hidden, down_weight):
    tok_rows = grad_out.shape[0]
    experts = lax.axis_size("expert")
    slots_all = saved_hidden.shape[3]
    capacity = slots_all // experts
    choices_flat = routes.reshape(-1)
    onehot = (choices_flat[:, None] == lax.iota(jnp.int32, experts)[None, :]).astype(jnp.int32)
    order_rank = jnp.sum((jnp.cumsum(onehot, axis=0) - onehot) * onehot, axis=-1)
    slot_of = (choices_flat * capacity + order_rank).reshape(tok_rows, 2)
    slot_ids = lax.iota(jnp.int32, experts * capacity)
    pick_first = (slot_of[None, :, 0] == slot_ids[:, None]).astype(jnp.bfloat16)
    pick_second = (slot_of[None, :, 1] == slot_ids[:, None]).astype(jnp.bfloat16)
    placer = pick_first + pick_second
    send_rows = jnp.dot(placer, grad_out, preferred_element_type=jnp.float32).astype(jnp.bfloat16)
    send_gate = (
        jnp.dot(pick_first, gate_weights[:, 0], preferred_element_type=jnp.float32)
        + jnp.dot(pick_second, gate_weights[:, 1], preferred_element_type=jnp.float32)
    ).astype(jnp.bfloat16)
    send_rows = send_rows.reshape(experts, capacity, send_rows.shape[-1])
    send_gate = send_gate.reshape(experts, capacity)
    recv_rows, recv_gate = (
        lax.all_to_all(send_rows, "expert", split_axis=0, concat_axis=0, tiled=True),
        lax.all_to_all(send_gate, "expert", split_axis=0, concat_axis=0, tiled=True),
    )
    rows_here = recv_rows.reshape(slots_all, recv_rows.shape[-1])
    gate_here = recv_gate.reshape(slots_all)
    weight = down_weight[0]
    gathered = lax.all_gather(rows_here, "etp", axis=1, tiled=True)
    raw_grad = contract_last(gathered, weight)
    gate_pre = saved_hidden[0, 0, 0].astype(jnp.float32)
    up_pre = saved_hidden[0, 0, 1].astype(jnp.float32)
    gate_col = gate_here.astype(jnp.float32)[:, None]
    sigmoid_val = jax.nn.sigmoid(gate_pre)
    silu_val = gate_pre * sigmoid_val
    act_grad = gate_col * raw_grad
    grad_gate = act_grad * up_pre * sigmoid_val * (1.0 + gate_pre * (1.0 - sigmoid_val))
    grad_up = act_grad * silu_val
    hidden_grad = jnp.stack([grad_gate, grad_up], axis=0).astype(jnp.bfloat16)[None, None]
    scaled = (gate_col * silu_val * up_pre).astype(jnp.bfloat16)
    summed = lax.psum_scatter(
        contract_first(gathered, scaled), "dp", scatter_dimension=0, tiled=True
    )
    weight_grad = summed.astype(jnp.bfloat16)[None]
    return (hidden_grad, weight_grad)


def solution(mesh):
    placed = (
        P(("dp", "expert"), "etp"),
        P(("dp", "expert"), None),
        P(("dp", "expert"), None),
        P("dp", "expert", None, None, "etp"),
        P("expert", "etp", None),
    )
    return jax.shard_map(
        per_device,
        mesh=mesh,
        in_specs=placed,
        out_specs=(P("dp", "expert", None, None, "etp"), P("expert", "dp", "etp")),
        check_vma=False,
    )
```

profile of v0, /device:TPU:7, one launch (start us, length us, event | category | flops | bytes accessed | tf_op | source)
XLA Modules:
  0.0 607.2 jit_solution(13538463245440196519)
XLA Ops:
  7.2 0.0 copy-start
  7.2 0.0 all-gather.2.cloned.1.call-start
  7.2 0.8 copy.17
  8.0 0.1 eq.45
  8.1 0.1 fusion.31
  8.2 0.2 reduce_window_sum.11
  8.4 0.2 select_reduce_fusion
  8.6 0.1 reduce_sum.12
  8.7 0.1 copy.18
  8.8 0.7 multiply_add_fusion
  9.5 0.0 copy-done
  9.5 0.2 convolution_convert_fusion
  9.7 15.6 %all_to_all.15 = bf16[8,32,384]{2,1,0:T(8,128)(2,1)} all-to-all(bf16[8,32,384]{2,1,0:T(8,128)(2,1)S(1)} %bitcast.47), channel_id=1, replica_groups=mesh['dp'=8,'expert'=8,'etp'=16] {'expert'}, dimensions={0} | all-to-all | bytes 393216 | tf_op jit(solution)/shard_map/all_to_all | solution.py:40
  25.2 0.0 all-gather.2.cloned.1.call-update
  25.3 0.0 reduce-scatter.2.cloned.1.call-start
  25.3 0.8 fusion.23
  26.1 0.8 fusion.21
  26.9 0.1 all_to_all.12
  27.0 9.4 %all_to_all.16 = bf16[8,1,32]{2,1,0:T(2,128)(2,1)S(1)} all-to-all(bf16[8,1,32]{2,1,0:T(2,128)(2,1)S(1)} %all_to_all.12), channel_id=1, replica_groups=mesh['dp'=8,'expert'=8,'etp'=16] {'expert'}, dimensions={0} | all-to-all | bytes 1024 | tf_op jit(solution)/shard_map/all_to_all | solution.py:41
  36.4 0.1 reshape.68
  36.5 99.8 %all-gather.2.cloned.1.call-done = bf16[256,6144]{1,0:T(8,128)(2,1)} async-done(((bf16[256,384]{1,0:T(8,128)(2,1)}), bf16[256,6144]{1,0:T(8,128)(2,1)}) %all-gather.2.cloned.1.call-update) | async-done | bytes 3145744 | tf_op jit(solution)/shard_map/all_gather | solution.py:46
  136.3 8.5 %fusion.14 = f32[6144,512]{1,0:T(8,128)} fusion(bf16[256,6144]{1,0:T(8,128)(2,1)} %all-gather.2.cloned.1.call-done, f32[256]{0:T(256)S(1)} %reshape.68, bf16[1,1,2,256,512]{4,3,2,1,0:T(8,128)(2,1)} %param.8), kind=kOutput, calls=%fused_computation.21 | convolution fusion | flops 1611792384 | bytes 16253952 | tf_op jit(solution)/shard_map/dot_general | solution.py:8
  144.9 0.0 copy-start.1
  144.9 0.0 reduce-scatter.2.cloned.1.call-update
  144.9 1.9 copy-done.1
  146.7 5.4 fusion.18
  152.1 0.8 pad_maximum_fusion
  153.0 445.0 %reduce-scatter.2.cloned.1.call-done = f32[768,512]{1,0:T(8,128)} async-done(((f32[6144,512]{1,0:T(8,128)}), f32[768,512]{1,0:T(8,128)}) %reduce-scatter.2.cloned.1.call-update) | async-done | bytes 1572880 | tf_op jit(solution)/shard_map/reduce_scatter | solution.py:58
  597.9 2.4 convert_bitcast_fusion
  (3 shorter events, 0.0 us)
Async XLA Ops:
  7.2 2.3 copy-start
  7.2 129.1 %all-gather.2.cloned.1.call-start = ((), (), s32[]{:S(2)}) async-start(), calls=%async_computation.3 | async-start | bytes 3342336 | tf_op jit(solution)/shard_map/all_gather | solution.py:46
  25.3 572.7 %reduce-scatter.2.cloned.1.call-start = ((), (), s32[]{:S(2)}) async-start(), calls=%async_computation.4 | async-start | bytes 14155776 | tf_op jit(solution)/shard_map/reduce_scatter | solution.py:58
  144.9 1.9 copy-start.1
Sparse Core Ops, SparseCore 0:
  25.4 110.8 all-gather.1
  145.0 452.8 reduce-scatter.1
where the time goes:
time: 609 us; the launch traced here: 607 us
  waiting for transfers between devices  545 us (89%)
  blocking collectives  24.9 us (4%)
  matrix products  15.7 us (3%)
  between operations  14.1 us (2%)
    reduce_scatter x1, waiting for transfers between devices, per_device(): lax.psum_scatter(contract_first(gathered, scaled), 'dp', scatter_dimensio...  445 us
    all_gather x1, waiting for transfers between devices, per_device(): gathered = lax.all_gather(rows_here, 'etp', axis=1, tiled=True)  99.8 us
    all_to_all x1, blocking collectives, per_device(): lax.all_to_all(send_rows, 'expert', split_axis=0, concat_axis=0, tiled=True)  15.6 us
  transfers between devices with their start and end apart: 2, of which 2 were waited for; matrix products, arithmetic and copies ran while one was open for 1% of the time, Pallas kernels for 0%

commit v1 on v0

v1 whole, which is shorter than its diff:
```python
import jax
import jax.numpy as jnp
from jax import lax
from jax.experimental import pallas as pl
from jax.experimental.pallas import tpu as pltpu
from jax.sharding import PartitionSpec as P

MESH = pl.DeviceIdType.MESH
BF16 = jnp.bfloat16
F32 = jnp.float32
NE = 8
NX = 4
NZ = 8
CAP = 32
PEERS_Y = (4, 3, 5, 2, 6, 1, 7)


def kernel(
    grad_ref, routes_ref, gates_ref, saved_ref, weight_hbm, hidden_ref, wgrad_ref,
    tok, place, ranks, picked, slots, gate_out, gate_in, weight, raw, fac_gate, fac_up, act,
    scaled, far_tok, far_ranks, far_picked, rows, total,
    w_sem, gate_s, gate_r, tok_up, tok_dn, tok_r, rank_s, rank_r, far_s, far_r, pick_s, pick_r,
    sib_s, sib_r, near_s, near_r, nsib_s, nsib_r, fpick_s, fpick_r, fsib_s, fsib_r,
    cross_s, sc_s, fsc_s, sc_r,
):
    dp = lax.axis_index("dp")
    y = lax.axis_index("expert")
    etp = lax.axis_index("etp")
    half, px = lax.div(dp, NX), lax.rem(dp, NX)
    zl, core = lax.div(etp, 2), lax.rem(etp, 2)
    other = 1 - half
    tokens, width = grad_ref.shape
    nslots = NE * CAP
    mine = pl.ds(pl.multiple_of(y * CAP, CAP), CAP)

    def at(dp_=None, y_=None, z_=None, core_=None):
        return {
            "dp": dp if dp_ is None else dp_,
            "expert": y if y_ is None else y_,
            "etp": (zl if z_ is None else z_) * 2 + (core if core_ is None else core_),
        }

    def y_peer(k):
        return lax.rem(y + k, NE)

    def x_peer(k):
        return lax.rem(px + k, NX)

    def far(x):
        return at(dp_=other * NX + x)

    def near(x):
        return at(dp_=half * NX + x)

    sibling = at(core_=1 - core)

    def remote(src, dst, send, recv, where):
        return pltpu.make_async_remote_copy(
            src_ref=src, dst_ref=dst, send_sem=send, recv_sem=recv, device_id=where, device_id_type=MESH
        )

    def drain(ref, sem):
        pltpu.make_async_copy(ref, ref, sem).wait()

    barrier = pltpu.get_barrier_semaphore()

    def greet(where):
        pl.semaphore_signal(barrier, inc=1, device_id=where, device_id_type=MESH)

    for x in range(NX):
        greet(far(x))
    for k in PEERS_Y:
        greet(at(y_=y_peer(k)))
    for k in (2, 1, 3):
        greet(near(x_peer(k)))
    greet(sibling)

    @pl.when(zl > 0)
    def _():
        greet(at(z_=zl - 1))

    @pl.when(zl < NZ - 1)
    def _():
        greet(at(z_=zl + 1))

    for j in range(2 * NZ):
        pltpu.make_async_copy(weight_hbm.at[:, pl.ds(j * width, width)], weight.at[j], w_sem).start()

    lane = lax.broadcasted_iota(jnp.int32, (tokens, 128), 1)
    first = routes_ref[:, 0:1] == lane
    second = routes_ref[:, 1:2] == lane
    named = jnp.where(first | second, 1.0, 0.0).astype(BF16)
    gates = gates_ref[...].astype(F32)
    token_gate = jnp.where(first, gates[:, 0:1], 0.0) + jnp.where(second, gates[:, 1:2], 0.0)
    r_id = lax.broadcasted_iota(jnp.int32, (tokens, 128), 0)
    after = jnp.where(r_id < lane, 1.0, 0.0).astype(BF16)
    same = jnp.where(r_id == lane, 1.0, 0.0).astype(BF16)
    contract_rows = (((0,), (0,)), ((), ()))
    earlier = lax.dot_general(named, after, contract_rows, preferred_element_type=F32)
    names = lax.dot_general(named, same, contract_rows, preferred_element_type=F32)
    ranks[...] = jnp.where(names > 0.5, earlier, -1.0)[0:16].astype(BF16)

    def build_place(source):
        table = source.astype(F32)
        slot = lax.broadcasted_iota(jnp.int32, (CAP, tokens), 0).astype(F32)
        for e in range(NE):
            hit = table[e:e + 1, 0:tokens] == slot
            place[e * CAP:(e + 1) * CAP, :] = jnp.where(hit, 1.0, 0.0).astype(BF16)

    build_place(ranks[...])
    in_slots = jnp.dot(place[...], token_gate.astype(BF16), preferred_element_type=F32)
    s_row = lax.broadcasted_iota(jnp.int32, (nslots, 128), 0)
    s_lane = lax.broadcasted_iota(jnp.int32, (nslots, 128), 1)
    own_gate = jnp.where(lax.div(s_row, CAP) == s_lane, in_slots, 0.0)
    own_gate = jnp.sum(own_gate, axis=1, keepdims=True)
    gate_out[...] = jnp.broadcast_to(own_gate, (nslots, 128)).astype(BF16)
    gate_in[mine, :] = gate_out[mine, :]
    tok[zl] = grad_ref[...]

    def pick(z):
        picked[z] = jnp.dot(place[...], tok[z], preferred_element_type=F32).astype(BF16)
        slots[z, core, mine, :] = picked[z, mine, :]

    def send_picked(z):
        for k in PEERS_Y:
            to = y_peer(k)
            there = pl.ds(pl.multiple_of(to * CAP, CAP), CAP)
            remote(picked.at[z, there], slots.at[z, core, mine], pick_s.at[z], pick_r.at[z], at(y_=to)).start()

    def send_far(z):
        @pl.when(lax.div(z, NX) == other)
        def _():
            remote(tok.at[z], far_tok.at[px], far_s.at[lax.rem(z, NX)], far_r.at[px], far(lax.rem(z, NX))).start()

    pick(zl)

    ends = jnp.where(zl > 0, 1, 0) + jnp.where(zl < NZ - 1, 1, 0)
    pl.semaphore_wait(barrier, 15 + ends)

    for k in PEERS_Y:
        to = y_peer(k)
        there = pl.ds(pl.multiple_of(to * CAP, CAP), CAP)
        remote(gate_out.at[there], gate_in.at[mine], gate_s, gate_r, at(y_=to)).start()

    @pl.when(zl < NZ - 1)
    def _():
        remote(tok.at[zl], tok.at[zl], tok_up.at[zl], tok_r.at[zl], at(z_=zl + 1)).start()

    @pl.when(zl > 0)
    def _():
        remote(tok.at[zl], tok.at[zl], tok_dn.at[zl], tok_r.at[zl], at(z_=zl - 1)).start()

    for x in range(NX):
        remote(ranks, far_ranks.at[px], rank_s.at[x], rank_r.at[px], far(x)).start()
    send_far(zl)
    send_picked(zl)

    gate_pre = saved_ref[0].astype(F32)
    up_pre = saved_ref[1].astype(F32)
    sig = jax.nn.sigmoid(gate_pre)
    silu = gate_pre * sig
    fac_gate[...] = up_pre * sig * (1.0 + gate_pre * (1.0 - sig))
    fac_up[...] = silu
    act[...] = silu * up_pre

    def nearest(k):
        short = jnp.minimum(zl, NZ - 1 - zl)
        step = lax.div(k + 1, 2)
        zigzag = jnp.where(lax.rem(k, 2) == 1, zl - step, zl + step)
        return jnp.where(k <= 2 * short, zigzag, jnp.where(zl < NZ // 2, k, NZ - 1 - k))

    def pass_tokens(k, carry):
        z = nearest(k)
        drain(tok.at[z], tok_r.at[z])

        @pl.when((z < zl) & (zl < NZ - 1))
        def _():
            remote(tok.at[z], tok.at[z], tok_up.at[z], tok_r.at[z], at(z_=zl + 1)).start()

        @pl.when((z > zl) & (zl > 0))
        def _():
            remote(tok.at[z], tok.at[z], tok_dn.at[z], tok_r.at[z], at(z_=zl - 1)).start()

        send_far(z)
        pick(z)
        send_picked(z)
        return carry

    lax.fori_loop(1, 4, pass_tokens, 0)

    drain(gate_in.at[0:nslots - CAP], gate_r)
    gate_col = gate_in[...].astype(F32)[:, 0:1]
    scaled[dp] = (gate_col * act[...]).astype(BF16)
    hrows = nslots // 2
    for h in range(2):
        part = scaled.at[dp, pl.ds(h * hrows, hrows)]
        remote(part, part, cross_s.at[h], sc_r.at[dp, h], far(px)).start()
    for k in (2, 1, 3):
        x = x_peer(k)
        for h in range(2):
            part = scaled.at[dp, pl.ds(h * hrows, hrows)]
            remote(part, part, sc_s.at[h, x], sc_r.at[dp, h], near(x)).start()

    lax.fori_loop(4, NZ, pass_tokens, 0)

    drain(weight, w_sem)
    raw[...] = jnp.zeros_like(raw)
    total[...] = jnp.zeros_like(total)

    def add_raw(z, c):
        raw[...] += lax.dot_general(
            slots[z, c], weight[2 * z + c], (((1,), (1,)), ((), ())), preferred_element_type=F32
        )

    def take_slots(k, carry):
        z = nearest(k)
        drain(slots.at[z, core, pl.ds(0, nslots - CAP)], pick_r.at[z])
        block = slots.at[z, core]
        remote(block, block, sib_s.at[z], sib_r.at[z], sibling).start()

        @pl.when((lax.div(z, NX) == half) & (z != dp))
        def _():
            x = lax.rem(z, NX)
            remote(block, rows.at[dp, core], near_s.at[x], near_r.at[px], near(x)).start()

        add_raw(z, core)

        @pl.when(k > 0)
        def _():
            before = nearest(jnp.maximum(k - 1, 0))
            drain(slots.at[before, 1 - core], sib_r.at[before])
            add_raw(before, 1 - core)

        return carry

    lax.fori_loop(0, 4, take_slots, 0)

    def take_far(q, carry):
        drain(far_ranks.at[q], rank_r.at[q])
        drain(far_tok.at[q], far_r.at[q])
        build_place(far_ranks[q])
        far_picked[q] = jnp.dot(place[...], far_tok[q], preferred_element_type=F32).astype(BF16)
        far_dp = other * NX + q
        rows[far_dp, core, mine, :] = far_picked[q, mine, :]
        for k in PEERS_Y:
            to = y_peer(k)
            there = pl.ds(pl.multiple_of(to * CAP, CAP), CAP)
            remote(
                far_picked.at[q, there], rows.at[far_dp, core, mine], fpick_s.at[q], fpick_r.at[q], at(y_=to)
            ).start()
        return carry

    lax.fori_loop(0, NX, take_far, 0)
    lax.fori_loop(4, 6, take_slots, 0)

    twin = other * NX + px
    for h in range(2):
        part = scaled.at[twin, pl.ds(h * hrows, hrows)]
        drain(part, sc_r.at[twin, h])
        for k in (2, 1, 3):
            x = x_peer(k)
            remote(part, part, fsc_s.at[h, x], sc_r.at[twin, h], near(x)).start()

    lax.fori_loop(6, NZ, take_slots, 0)
    last = nearest(NZ - 1)
    drain(slots.at[last, 1 - core], sib_r.at[last])
    add_raw(last, 1 - core)
    gated = gate_in[...].astype(F32)[:, 0:1] * raw[...]
    hidden_ref[0] = (gated * fac_gate[...]).astype(BF16)
    hidden_ref[1] = (gated * fac_up[...]).astype(BF16)

    def add_total(c, left, right):
        total[c] += lax.dot_general(left, right, contract_rows, preferred_element_type=F32)

    for c in range(2):
        add_total(c, slots[dp, c], scaled[dp])

    def near_arrive(k, carry):
        x = x_peer(k)
        src = half * NX + x
        block = rows.at[src, core]
        drain(block, near_r.at[x])
        remote(block, block, nsib_s.at[x], nsib_r.at[x], sibling).start()
        return carry

    lax.fori_loop(1, NX, near_arrive, 0)

    def near_add(k, carry):
        x = x_peer(k)
        src = half * NX + x
        for h in range(2):
            drain(scaled.at[src, pl.ds(h * hrows, hrows)], sc_r.at[src, h])
        add_total(core, rows[src, core], scaled[src])
        drain(rows.at[src, 1 - core], nsib_r.at[x])
        add_total(1 - core, rows[src, 1 - core], scaled[src])
        return carry

    lax.fori_loop(1, NX, near_add, 0)

    def far_arrive(q, carry):
        src = other * NX + q
        drain(rows.at[src, core, pl.ds(0, nslots - CAP)], fpick_r.at[q])
        block = rows.at[src, core]
        remote(block, block, fsib_s.at[q], fsib_r.at[q], sibling).start()

        @pl.when(q != px)
        def _():
            for h in range(2):
                drain(scaled.at[src, pl.ds(h * hrows, hrows)], sc_r.at[src, h])

        add_total(core, rows[src, core], scaled[src])
        drain(rows.at[src, 1 - core], fsib_r.at[q])
        add_total(1 - core, rows[src, 1 - core], scaled[src])
        return carry

    lax.fori_loop(0, NX, far_arrive, 0)
    wgrad_ref[0:width, :] = total[0].astype(BF16)
    wgrad_ref[width:2 * width, :] = total[1].astype(BF16)

    drain(gate_out.at[0:nslots - CAP], gate_s)
    for x in range(NX):
        drain(ranks, rank_s.at[x])

    def sent_blocks(z, carry):
        @pl.when((z <= zl) & (zl < NZ - 1))
        def _():
            drain(tok.at[z], tok_up.at[z])

        @pl.when((z >= zl) & (zl > 0))
        def _():
            drain(tok.at[z], tok_dn.at[z])

        drain(picked.at[z, pl.ds(0, nslots - CAP)], pick_s.at[z])
        drain(slots.at[z, core], sib_s.at[z])
        return carry

    lax.fori_loop(0, NZ, sent_blocks, 0)

    def sent_parts(q, carry):
        drain(tok.at[0], far_s.at[q])
        drain(far_picked.at[q, pl.ds(0, nslots - CAP)], fpick_s.at[q])
        drain(rows.at[q, core], fsib_s.at[q])

        @pl.when(q != px)
        def _():
            drain(rows.at[q, core], near_s.at[q])
            drain(rows.at[q, core], nsib_s.at[q])
            for h in range(2):
                drain(scaled.at[q, pl.ds(0, hrows)], sc_s.at[h, q])
                drain(scaled.at[q, pl.ds(0, hrows)], fsc_s.at[h, q])

        return carry

    lax.fori_loop(0, NX, sent_parts, 0)
    for h in range(2):
        drain(scaled.at[dp, pl.ds(0, hrows)], cross_s.at[h])


def per_device(grad_out, routes, gate_weights, saved_hidden, down_weight):
    tokens, width = grad_out.shape
    nslots, units = saved_hidden.shape[3:]
    dma = pltpu.SemaphoreType.DMA
    vmem = pl.BlockSpec(memory_space=pltpu.VMEM)
    hidden_grad, weight_grad = pl.pallas_call(
        kernel,
        out_shape=(
            jax.ShapeDtypeStruct((2, nslots, units), BF16),
            jax.ShapeDtypeStruct((2 * width, units), BF16),
        ),
        in_specs=[vmem, vmem, vmem, vmem, pl.BlockSpec(memory_space=pl.ANY)],
        out_specs=(vmem, vmem),
        scratch_shapes=[
            pltpu.VMEM((NZ, tokens, width), BF16),
            pltpu.VMEM((nslots, tokens), BF16),
            pltpu.VMEM((16, 128), BF16),
            pltpu.VMEM((NZ, nslots, width), BF16),
            pltpu.VMEM((NZ, 2, nslots, width), BF16),
            pltpu.VMEM((nslots, 128), BF16),
            pltpu.VMEM((nslots, 128), BF16),
            pltpu.VMEM((2 * NZ, units, width), BF16),
            pltpu.VMEM((nslots, units), F32),
            pltpu.VMEM((nslots, units), F32),
            pltpu.VMEM((nslots, units), F32),
            pltpu.VMEM((nslots, units), F32),
            pltpu.VMEM((2 * NX, nslots, units), BF16),
            pltpu.VMEM((NX, tokens, width), BF16),
            pltpu.VMEM((NX, 16, 128), BF16),
            pltpu.VMEM((NX, nslots, width), BF16),
            pltpu.VMEM((2 * NX, 2, nslots, width), BF16),
            pltpu.VMEM((2, width, units), F32),
            dma(()),
            dma(()), dma(()),
            dma((NZ,)), dma((NZ,)), dma((NZ,)),
            dma((NX,)), dma((NX,)),
            dma((NX,)), dma((NX,)),
            dma((NZ,)), dma((NZ,)),
            dma((NZ,)), dma((NZ,)),
            dma((NX,)), dma((NX,)),
            dma((NX,)), dma((NX,)),
            dma((NX,)), dma((NX,)),
            dma((NX,)), dma((NX,)),
            dma((2,)), dma((2, NX)), dma((2, NX)), dma((2 * NX, 2)),
        ],
        compiler_params=pltpu.CompilerParams(
            collective_id=0, has_side_effects=True, vmem_limit_bytes=56 * 2**20
        ),
        name="moe_backward",
    )(grad_out, routes, gate_weights, saved_hidden[0, 0], down_weight[0])
    return hidden_grad[None, None], weight_grad[None]


def solution(mesh):
    placed = (
        P(("dp", "expert"), "etp"),
        P(("dp", "expert"), None),
        P(("dp", "expert"), None),
        P("dp", "expert", None, None, "etp"),
        P("expert", "etp", None),
    )
    return jax.shard_map(
        per_device,
        mesh=mesh,
        in_specs=placed,
        out_specs=(P("dp", "expert", None, None, "etp"), P("expert", "dp", "etp")),
        check_vma=False,
    )
```

time: 609 us -> 122 us (0.20)
  waiting for transfers between devices: 545 us -> 0 us
  Pallas kernels: 0 us -> 114 us
  blocking collectives: 24.9 us -> 0 us
  matrix products: 15.7 us -> 0 us
  between operations: 14.1 us -> 0.64 us
    reduce_scatter x1 -> x0, waiting for transfers between devices: 445 us -> none  [per_device(): lax.psum_scatter(contract_first(gathered, scaled), 'dp', scatter_dimensio...]
    pallas_call x0 -> x1, Pallas kernels: none -> 114 us  [per_device(): pl.pallas_call(kernel, out_shape=(jax.ShapeDtypeStruct((2, nslots, units)...]
    all_gather x1 -> x0, waiting for transfers between devices: 99.8 us -> none  [per_device(): gathered = lax.all_gather(rows_here, 'etp', axis=1, tiled=True)]
    all_to_all x2 -> x0, blocking collectives: 24.9 us -> none  [the longest x1 15.6 us: per_device(): lax.all_to_all(send_rows, 'expert', split_axis=0, concat_axis=0, tiled=True)]
    dot_general x5 -> x0, matrix products: 15.7 us -> none  [the longest x1 8.53 us: contract_first(): lax.dot_general(left, right, (((0,), (0,)), ((), ())), preferred_element_...]
  transfers between devices with their start and end apart: 2 -> 0, of which waited for: 2 -> 0; matrix products, arithmetic and copies ran while one was open for 1% -> 0% of each run, Pallas kernels for 0% -> 0%
where the time goes in v1:
time: 122 us; the launch traced here: 121 us
  Pallas kernels  114 us (93%)
  local copies, waits for them, and re-layouts  6.67 us (5%)
    pallas_call x1, Pallas kernels, per_device(): pl.pallas_call(kernel, out_shape=(jax.ShapeDtypeStruct((2, nslots, units)...  114 us
    unnamed x4, local copies, waits for them, and re-layouts  6.67 us

profile of v1, /device:TPU:7, one launch (start us, length us, event | category | flops | bytes accessed | tf_op | source)
XLA Modules:
  0.0 121.4 jit_solution(8125206161277355848)
XLA Ops:
  0.6 1.4 %copy.8.gates_ref = bf16[64,2]{1,0:T(8,128)(2,1)} copy(bf16[64,2]{0,1:T(2,128)(2,1)} %param.7) | data formatting | bytes 512 | tf_op args[2]
  2.0 1.4 %copy.7.routes_ref = s32[64,2]{1,0:T(8,128)} copy(s32[64,2]{0,1:T(2,128)} %param.6) | data formatting | bytes 1024 | tf_op args[1]
  3.4 114.1 %moe_backward.1 = (bf16[2,256,512]{2,1,0:T(8,128)(2,1)}, bf16[768,512]{1,0:T(8,128)(2,1)}) custom-call(bf16[64,384]{1,0:T(8,128)(2,1)} %grad_ref.1, s32[64,2]{1,0:T(8,128)} %copy.7.routes_ref, bf16[64,2]{1,0:T(8,128)(2,1)} %copy.8.gates_ref, bf16[2,256,512]{2,1,0:T(8,128)(2,1)} %bitcast.7, bf16[512,6144]{1,0:T(8,128)(2,1)} %bitcast.4), custom_call_target="tpu_custom_call" | custom-call | tf_op jit(solution)/shard_map/moe_backward/pallas_call | solution.py:364
  117.5 1.9 %copy.11 = bf16[1,1,2,256,512]{4,3,2,1,0:T(8,128)(2,1)} copy(bf16[1,1,2,256,512]{4,3,2,1,0:T(8,128)(2,1)} %bitcast.6) | data formatting | bytes 1048576
  119.4 2.1 %copy.12 = bf16[1,768,512]{2,1,0:T(8,128)(2,1)} copy(bf16[1,768,512]{2,1,0:T(8,128)(2,1)} %bitcast.5) | data formatting | bytes 1572864

commit v2 on v1

--- a/solution.py
+++ b/solution.py
@@ -12,16 +12,18 @@
 NX = 4
 NZ = 8
 CAP = 32
+PARTS = 8
+FIRST = 3
 PEERS_Y = (4, 3, 5, 2, 6, 1, 7)
 
 
 def kernel(
     grad_ref, routes_ref, gates_ref, saved_ref, weight_hbm, hidden_ref, wgrad_ref,
-    tok, place, ranks, picked, slots, gate_out, gate_in, weight, raw, fac_gate, fac_up, act,
-    scaled, far_tok, far_ranks, far_picked, rows, total,
-    w_sem, gate_s, gate_r, tok_up, tok_dn, tok_r, rank_s, rank_r, far_s, far_r, pick_s, pick_r,
+    tok, place, far_src, picked, slots, gate_out, gate_in, weight, raw, fac_gate, fac_up, act,
+    scaled, far_tok, far_picked, rows, total,
+    w_sem, gate_s, gate_r, tok_up, tok_dn, tok_r, far_s, far_r, far_up, far_dn, pick_s, pick_r,
     sib_s, sib_r, near_s, near_r, nsib_s, nsib_r, fpick_s, fpick_r, fsib_s, fsib_r,
-    cross_s, sc_s, fsc_s, sc_r,
+    cross_s, cross_r, sc_s, sc_r, fsc_s, fsc_r,
 ):
     dp = lax.axis_index("dp")
     y = lax.axis_index("expert")
@@ -67,8 +69,17 @@
     def greet(where):
         pl.semaphore_signal(barrier, inc=1, device_id=where, device_id_type=MESH)
 
-    for x in range(NX):
-        greet(far(x))
+    far_source = lax.div(zl, NX) == other
+    far_target = zl == jnp.where(half == 0, NZ // 2, NZ // 2 - 1)
+    far_above = zl >= jnp.where(half == 0, NZ // 2, NZ // 2 - 1)
+    far_below = zl <= jnp.where(half == 0, NZ // 2, NZ // 2 - 1)
+
+    @pl.when(far_target)
+    def _():
+        for x in range(NX):
+            greet(at(dp_=other * NX + x, z_=dp))
+
+    greet(far(px))
     for k in PEERS_Y:
         greet(at(y_=y_peer(k)))
     for k in (2, 1, 3):
@@ -86,36 +97,36 @@
     for j in range(2 * NZ):
         pltpu.make_async_copy(weight_hbm.at[:, pl.ds(j * width, width)], weight.at[j], w_sem).start()
 
-    lane = lax.broadcasted_iota(jnp.int32, (tokens, 128), 1)
-    first = routes_ref[:, 0:1] == lane
-    second = routes_ref[:, 1:2] == lane
-    named = jnp.where(first | second, 1.0, 0.0).astype(BF16)
+    contract_rows = (((0,), (0,)), ((), ()))
+
+    expert_id = lax.broadcasted_iota(jnp.int32, (16, tokens), 0)
+    first = routes_ref[0:1, :] == expert_id
+    second = routes_ref[1:2, :] == expert_id
+    named = jnp.where(first | second, 1.0, 0.0)
     gates = gates_ref[...].astype(F32)
-    token_gate = jnp.where(first, gates[:, 0:1], 0.0) + jnp.where(second, gates[:, 1:2], 0.0)
-    r_id = lax.broadcasted_iota(jnp.int32, (tokens, 128), 0)
-    after = jnp.where(r_id < lane, 1.0, 0.0).astype(BF16)
-    same = jnp.where(r_id == lane, 1.0, 0.0).astype(BF16)
-    contract_rows = (((0,), (0,)), ((), ()))
-    earlier = lax.dot_general(named, after, contract_rows, preferred_element_type=F32)
-    names = lax.dot_general(named, same, contract_rows, preferred_element_type=F32)
-    ranks[...] = jnp.where(names > 0.5, earlier, -1.0)[0:16].astype(BF16)
-
-    def build_place(source):
-        table = source.astype(F32)
-        slot = lax.broadcasted_iota(jnp.int32, (CAP, tokens), 0).astype(F32)
+    token_gate = jnp.where(first, gates[0:1, :], 0.0) + jnp.where(second, gates[1:2, :], 0.0)
+    row = lax.broadcasted_iota(jnp.int32, (tokens, tokens), 0)
+    col = lax.broadcasted_iota(jnp.int32, (tokens, tokens), 1)
+    after = jnp.where(row < col, 1.0, 0.0).astype(BF16)
+    earlier = jnp.dot(named.astype(BF16), after, preferred_element_type=F32)
+    table = jnp.where(named > 0.5, earlier, -1.0)
+    slot = lax.broadcasted_iota(jnp.int32, (CAP, tokens), 0).astype(F32)
+
+    def build_place(table):
         for e in range(NE):
-            hit = table[e:e + 1, 0:tokens] == slot
-            place[e * CAP:(e + 1) * CAP, :] = jnp.where(hit, 1.0, 0.0).astype(BF16)
-
-    build_place(ranks[...])
-    in_slots = jnp.dot(place[...], token_gate.astype(BF16), preferred_element_type=F32)
-    s_row = lax.broadcasted_iota(jnp.int32, (nslots, 128), 0)
-    s_lane = lax.broadcasted_iota(jnp.int32, (nslots, 128), 1)
-    own_gate = jnp.where(lax.div(s_row, CAP) == s_lane, in_slots, 0.0)
-    own_gate = jnp.sum(own_gate, axis=1, keepdims=True)
-    gate_out[...] = jnp.broadcast_to(own_gate, (nslots, 128)).astype(BF16)
+            hit = jnp.where(table[e:e + 1, :] == slot, 1.0, 0.0)
+            place[e * CAP:(e + 1) * CAP, :] = hit.astype(BF16)
+
+    for e in range(NE):
+        hit = jnp.where(table[e:e + 1, :] == slot, 1.0, 0.0)
+        place[e * CAP:(e + 1) * CAP, :] = hit.astype(BF16)
+        gate = jnp.sum(hit * token_gate[e:e + 1, :], axis=1, keepdims=True)
+        gate_out[e * CAP:(e + 1) * CAP, :] = jnp.broadcast_to(gate, (CAP, 128)).astype(BF16)
+
     gate_in[mine, :] = gate_out[mine, :]
     tok[zl] = grad_ref[...]
+    far_src[0:tokens, :] = grad_ref[...]
+    far_src[tokens:tokens + 16, 0:tokens] = table.astype(BF16)
 
     def pick(z):
         picked[z] = jnp.dot(place[...], tok[z], preferred_element_type=F32).astype(BF16)
@@ -127,15 +138,10 @@
             there = pl.ds(pl.multiple_of(to * CAP, CAP), CAP)
             remote(picked.at[z, there], slots.at[z, core, mine], pick_s.at[z], pick_r.at[z], at(y_=to)).start()
 
-    def send_far(z):
-        @pl.when(lax.div(z, NX) == other)
-        def _():
-            remote(tok.at[z], far_tok.at[px], far_s.at[lax.rem(z, NX)], far_r.at[px], far(lax.rem(z, NX))).start()
-
     pick(zl)
 
     ends = jnp.where(zl > 0, 1, 0) + jnp.where(zl < NZ - 1, 1, 0)
-    pl.semaphore_wait(barrier, 15 + ends)
+    pl.semaphore_wait(barrier, 12 + ends + jnp.where(far_source, 1, 0))
 
     for k in PEERS_Y:
         to = y_peer(k)
@@ -150,9 +156,11 @@
     def _():
         remote(tok.at[zl], tok.at[zl], tok_dn.at[zl], tok_r.at[zl], at(z_=zl - 1)).start()
 
-    for x in range(NX):
-        remote(ranks, far_ranks.at[px], rank_s.at[x], rank_r.at[px], far(x)).start()
-    send_far(zl)
+    @pl.when(far_source)
+    def _():
+        land = jnp.where(other == 0, NZ // 2, NZ // 2 - 1)
+        remote(far_src, far_tok.at[px], far_s, far_r.at[px], at(dp_=zl, z_=land)).start()
+
     send_picked(zl)
 
     gate_pre = saved_ref[0].astype(F32)
@@ -169,39 +177,83 @@
         zigzag = jnp.where(lax.rem(k, 2) == 1, zl - step, zl + step)
         return jnp.where(k <= 2 * short, zigzag, jnp.where(zl < NZ // 2, k, NZ - 1 - k))
 
-    def pass_tokens(k, carry):
-        z = nearest(k)
-        drain(tok.at[z], tok_r.at[z])
-
-        @pl.when((z < zl) & (zl < NZ - 1))
-        def _():
-            remote(tok.at[z], tok.at[z], tok_up.at[z], tok_r.at[z], at(z_=zl + 1)).start()
-
-        @pl.when((z > zl) & (zl > 0))
-        def _():
-            remote(tok.at[z], tok.at[z], tok_dn.at[z], tok_r.at[z], at(z_=zl - 1)).start()
-
-        send_far(z)
-        pick(z)
-        send_picked(z)
-        return carry
-
-    lax.fori_loop(1, 4, pass_tokens, 0)
+    def pass_far(q, carry):
+        block = far_tok.at[q]
+        drain(block, far_r.at[q])
+
+        @pl.when(far_above & (zl < NZ - 1))
+        def _():
+            remote(block, block, far_up.at[q], far_r.at[q], at(z_=zl + 1)).start()
+
+        @pl.when(far_below & (zl > 0))
+        def _():
+            remote(block, block, far_dn.at[q], far_r.at[q], at(z_=zl - 1)).start()
+
+        return carry
+
+    part_rows = nslots // PARTS
+
+    def part_of(where, h):
+        return scaled.at[where, pl.ds(pl.multiple_of(h * part_rows, part_rows), part_rows)]
+
+    def start_cross(h):
+        remote(part_of(dp, h), part_of(dp, h), cross_s.at[h], cross_r.at[h], far(px)).start()
+
+    far_step = 2 + jnp.abs(zl - jnp.where(half == 0, NZ // 2, NZ // 2 - 1))
+
+    def pass_tokens(t, carry):
+        below, above = zl - t, zl + t
+
+        @pl.when(below >= 0)
+        def _():
+            block = tok.at[below]
+            drain(block, tok_r.at[below])
+
+            @pl.when(zl < NZ - 1)
+            def _():
+                remote(block, block, tok_up.at[below], tok_r.at[below], at(z_=zl + 1)).start()
+
+        @pl.when(above < NZ)
+        def _():
+            block = tok.at[above]
+            drain(block, tok_r.at[above])
+
+            @pl.when(zl > 0)
+            def _():
+                remote(block, block, tok_dn.at[above], tok_r.at[above], at(z_=zl - 1)).start()
+
+        @pl.when(below >= 0)
+        def _():
+            pick(below)
+            send_picked(below)
+
+        @pl.when(above < NZ)
+        def _():
+            pick(above)
+            send_picked(above)
+
+        @pl.when(t >= FIRST)
+        def _():
+            start_cross(t - FIRST)
+
+        @pl.when(t == far_step)
+        def _():
+            lax.fori_loop(0, NX, pass_far, 0)
+
+        return carry
+
+    lax.fori_loop(1, FIRST, pass_tokens, 0)
 
     drain(gate_in.at[0:nslots - CAP], gate_r)
     gate_col = gate_in[...].astype(F32)[:, 0:1]
     scaled[dp] = (gate_col * act[...]).astype(BF16)
-    hrows = nslots // 2
-    for h in range(2):
-        part = scaled.at[dp, pl.ds(h * hrows, hrows)]
-        remote(part, part, cross_s.at[h], sc_r.at[dp, h], far(px)).start()
     for k in (2, 1, 3):
         x = x_peer(k)
-        for h in range(2):
-            part = scaled.at[dp, pl.ds(h * hrows, hrows)]
-            remote(part, part, sc_s.at[h, x], sc_r.at[dp, h], near(x)).start()
-
-    lax.fori_loop(4, NZ, pass_tokens, 0)
+        remote(scaled.at[dp], scaled.at[dp], sc_s.at[x], sc_r.at[px], near(x)).start()
+
+    lax.fori_loop(FIRST, NZ, pass_tokens, 0)
+    for h in range(NZ - FIRST, PARTS):
+        start_cross(h)
 
     drain(weight, w_sem)
     raw[...] = jnp.zeros_like(raw)
@@ -233,13 +285,11 @@
 
         return carry
 
-    lax.fori_loop(0, 4, take_slots, 0)
-
     def take_far(q, carry):
-        drain(far_ranks.at[q], rank_r.at[q])
-        drain(far_tok.at[q], far_r.at[q])
-        build_place(far_ranks[q])
-        far_picked[q] = jnp.dot(place[...], far_tok[q], preferred_element_type=F32).astype(BF16)
+        build_place(far_tok[q, tokens:tokens + 16, 0:tokens].astype(F32))
+        far_picked[q] = jnp.dot(
+            place[...], far_tok[q, 0:tokens, :], preferred_element_type=F32
+        ).astype(BF16)
         far_dp = other * NX + q
         rows[far_dp, core, mine, :] = far_picked[q, mine, :]
         for k in PEERS_Y:
@@ -251,17 +301,23 @@
         return carry
 
     lax.fori_loop(0, NX, take_far, 0)
-    lax.fori_loop(4, 6, take_slots, 0)
+    lax.fori_loop(0, 6, take_slots, 0)
 
     twin = other * NX + px
-    for h in range(2):
-        part = scaled.at[twin, pl.ds(h * hrows, hrows)]
-        drain(part, sc_r.at[twin, h])
+
+    def pass_part(h):
+        part = scaled.at[twin, pl.ds(2 * h * part_rows, 2 * part_rows)]
+        for i in range(2):
+            drain(part_of(twin, 2 * h + i), cross_r.at[2 * h + i])
         for k in (2, 1, 3):
             x = x_peer(k)
-            remote(part, part, fsc_s.at[h, x], sc_r.at[twin, h], near(x)).start()
-
-    lax.fori_loop(6, NZ, take_slots, 0)
+            remote(part, part, fsc_s.at[x], fsc_r.at[px], near(x)).start()
+
+    pass_part(0)
+    take_slots(6, 0)
+    pass_part(1)
+    take_slots(7, 0)
+    pass_part(2)
     last = nearest(NZ - 1)
     drain(slots.at[last, 1 - core], sib_r.at[last])
     add_raw(last, 1 - core)
@@ -288,25 +344,29 @@
     def near_add(k, carry):
         x = x_peer(k)
         src = half * NX + x
-        for h in range(2):
-            drain(scaled.at[src, pl.ds(h * hrows, hrows)], sc_r.at[src, h])
+        drain(scaled.at[src], sc_r.at[x])
         add_total(core, rows[src, core], scaled[src])
         drain(rows.at[src, 1 - core], nsib_r.at[x])
         add_total(1 - core, rows[src, 1 - core], scaled[src])
         return carry
 
     lax.fori_loop(1, NX, near_add, 0)
+
+    pass_part(3)
 
     def far_arrive(q, carry):
         src = other * NX + q
         drain(rows.at[src, core, pl.ds(0, nslots - CAP)], fpick_r.at[q])
         block = rows.at[src, core]
         remote(block, block, fsib_s.at[q], fsib_r.at[q], sibling).start()
+        return carry
+
+    def far_add(q, carry):
+        src = other * NX + q
 
         @pl.when(q != px)
         def _():
-            for h in range(2):
-                drain(scaled.at[src, pl.ds(h * hrows, hrows)], sc_r.at[src, h])
+            drain(scaled.at[src], fsc_r.at[q])
 
         add_total(core, rows[src, core], scaled[src])
         drain(rows.at[src, 1 - core], fsib_r.at[q])
@@ -314,12 +374,15 @@
         return carry
 
     lax.fori_loop(0, NX, far_arrive, 0)
+    lax.fori_loop(0, NX, far_add, 0)
     wgrad_ref[0:width, :] = total[0].astype(BF16)
     wgrad_ref[width:2 * width, :] = total[1].astype(BF16)
 
     drain(gate_out.at[0:nslots - CAP], gate_s)
-    for x in range(NX):
-        drain(ranks, rank_s.at[x])
+
+    @pl.when(far_source)
+    def _():
+        drain(far_src, far_s)
 
     def sent_blocks(z, carry):
         @pl.when((z <= zl) & (zl < NZ - 1))
@@ -337,7 +400,14 @@
     lax.fori_loop(0, NZ, sent_blocks, 0)
 
     def sent_parts(q, carry):
-        drain(tok.at[0], far_s.at[q])
+        @pl.when(far_above & (zl < NZ - 1))
+        def _():
+            drain(far_tok.at[q], far_up.at[q])
+
+        @pl.when(far_below & (zl > 0))
+        def _():
+            drain(far_tok.at[q], far_dn.at[q])
+
         drain(far_picked.at[q, pl.ds(0, nslots - CAP)], fpick_s.at[q])
         drain(rows.at[q, core], fsib_s.at[q])
 
@@ -345,15 +415,19 @@
         def _():
             drain(rows.at[q, core], near_s.at[q])
             drain(rows.at[q, core], nsib_s.at[q])
-            for h in range(2):
-                drain(scaled.at[q, pl.ds(0, hrows)], sc_s.at[h, q])
-                drain(scaled.at[q, pl.ds(0, hrows)], fsc_s.at[h, q])
+            drain(scaled.at[q], sc_s.at[q])
+            drain(scaled.at[q], fsc_s.at[q])
 
         return carry
 
     lax.fori_loop(0, NX, sent_parts, 0)
-    for h in range(2):
-        drain(scaled.at[dp, pl.ds(0, hrows)], cross_s.at[h])
+    for h in range(PARTS):
+        drain(part_of(dp, h), cross_s.at[h])
+
+
+def hand_over(hidden_in, wgrad_in, hidden_out, wgrad_out):
+    hidden_out[...] = hidden_in[...]
+    wgrad_out[...] = wgrad_in[...]
 
 
 def per_device(grad_out, routes, gate_weights, saved_hidden, down_weight):
@@ -372,7 +446,7 @@
         scratch_shapes=[
             pltpu.VMEM((NZ, tokens, width), BF16),
             pltpu.VMEM((nslots, tokens), BF16),
-            pltpu.VMEM((16, 128), BF16),
+            pltpu.VMEM((tokens + 16, width), BF16),
             pltpu.VMEM((NZ, nslots, width), BF16),
             pltpu.VMEM((NZ, 2, nslots, width), BF16),
             pltpu.VMEM((nslots, 128), BF16),
@@ -383,29 +457,38 @@
             pltpu.VMEM((nslots, units), F32),
             pltpu.VMEM((nslots, units), F32),
             pltpu.VMEM((2 * NX, nslots, units), BF16),
-            pltpu.VMEM((NX, tokens, width), BF16),
-            pltpu.VMEM((NX, 16, 128), BF16),
+            pltpu.VMEM((NX, tokens + 16, width), BF16),
             pltpu.VMEM((NX, nslots, width), BF16),
             pltpu.VMEM((2 * NX, 2, nslots, width), BF16),
             pltpu.VMEM((2, width, units), F32),
             dma(()),
             dma(()), dma(()),
             dma((NZ,)), dma((NZ,)), dma((NZ,)),
-            dma((NX,)), dma((NX,)),
-            dma((NX,)), dma((NX,)),
+            dma(()), dma((NX,)), dma((NX,)), dma((NX,)),
             dma((NZ,)), dma((NZ,)),
             dma((NZ,)), dma((NZ,)),
             dma((NX,)), dma((NX,)),
             dma((NX,)), dma((NX,)),
             dma((NX,)), dma((NX,)),
             dma((NX,)), dma((NX,)),
-            dma((2,)), dma((2, NX)), dma((2, NX)), dma((2 * NX, 2)),
+            dma((PARTS,)), dma((PARTS,)),
+            dma((NX,)), dma((NX,)), dma((NX,)), dma((NX,)),
         ],
         compiler_params=pltpu.CompilerParams(
             collective_id=0, has_side_effects=True, vmem_limit_bytes=56 * 2**20
         ),
         name="moe_backward",
-    )(grad_out, routes, gate_weights, saved_hidden[0, 0], down_weight[0])
+    )(grad_out, routes.T, gate_weights.T, saved_hidden[0, 0], down_weight[0])
+    hidden_grad, weight_grad = pl.pallas_call(
+        hand_over,
+        out_shape=(
+            jax.ShapeDtypeStruct(hidden_grad.shape, BF16),
+            jax.ShapeDtypeStruct(weight_grad.shape, BF16),
+        ),
+        in_specs=[vmem, vmem],
+        out_specs=(vmem, vmem),
+        name="hand_over",
+    )(hidden_grad, weight_grad)
     return hidden_grad[None, None], weight_grad[None]
 
 

time: 122 us -> 102 us (0.84)
  the two profiles are of different devices: /device:TPU:7 before, /device:TPU:15 now
where the time goes in v2:
time: 102 us
  Pallas kernels  101 us (99%)
    pallas_call x1, Pallas kernels, per_device(): pl.pallas_call(kernel, out_shape=(jax.ShapeDtypeStruct((2, nslots, units)...  98.5 us
    pallas_call x1, Pallas kernels, per_device(): pl.pallas_call(hand_over, out_shape=(jax.ShapeDtypeStruct(hidden_grad.sha...  2.38 us

profile of v2, /device:TPU:15, one launch (start us, length us, event | category | flops | bytes accessed | tf_op | source)
XLA Modules:
  0.0 101.5 jit_solution(14446147842588824514)
XLA Ops:
  0.6 98.5 %moe_backward.1 = (bf16[2,256,512]{2,1,0:T(8,128)(2,1)}, bf16[768,512]{1,0:T(8,128)(2,1)}) custom-call(bf16[64,384]{1,0:T(8,128)(2,1)} %grad_ref.1, s32[2,64]{1,0:T(2,128)} %bitcast.8, bf16[2,64]{1,0:T(2,128)(2,1)} %bitcast.9, bf16[2,256,512]{2,1,0:T(8,128)(2,1)} %bitcast.7, bf16[512,6144]{1,0:T(8,128)(2,1)} %bitcast.6), custom_call_target="tpu_custom_call" | custom-call | tf_op jit(solution)/shard_map/moe_backward/pallas_call | solution.py:438
  99.1 2.4 %hand_over.1 = (bf16[2,256,512]{2,1,0:T(8,128)(2,1)}, bf16[768,512]{1,0:T(8,128)(2,1)}) custom-call(bf16[2,256,512]{2,1,0:T(8,128)(2,1)} %get-tuple-element.6.hidden_in, bf16[768,512]{1,0:T(8,128)(2,1)} %get-tuple-element.7.wgrad_in), custom_call_target="tpu_custom_call" | custom-call | tf_op jit(solution)/shard_map/hand_over/pallas_call | solution.py:482

commit v3 on v2

--- a/solution.py
+++ b/solution.py
@@ -12,18 +12,17 @@
 NX = 4
 NZ = 8
 CAP = 32
-PARTS = 8
-FIRST = 3
+PARTS = 4
 PEERS_Y = (4, 3, 5, 2, 6, 1, 7)
 
 
 def kernel(
     grad_ref, routes_ref, gates_ref, saved_ref, weight_hbm, hidden_ref, wgrad_ref,
     tok, place, far_src, picked, slots, gate_out, gate_in, weight, raw, fac_gate, fac_up, act,
-    scaled, far_tok, far_picked, rows, total,
+    scaled, hop, far_tok, far_picked, rows, total,
     w_sem, gate_s, gate_r, tok_up, tok_dn, tok_r, far_s, far_r, far_up, far_dn, pick_s, pick_r,
     sib_s, sib_r, near_s, near_r, nsib_s, nsib_r, fpick_s, fpick_r, fsib_s, fsib_r,
-    cross_s, cross_r, sc_s, sc_r, fsc_s, fsc_r,
+    hop_s, hop_r, sc_s, sc_r, fsc_s, fsc_r,
 ):
     dp = lax.axis_index("dp")
     y = lax.axis_index("expert")
@@ -48,9 +47,6 @@
     def x_peer(k):
         return lax.rem(px + k, NX)
 
-    def far(x):
-        return at(dp_=other * NX + x)
-
     def near(x):
         return at(dp_=half * NX + x)
 
@@ -79,20 +75,18 @@
         for x in range(NX):
             greet(at(dp_=other * NX + x, z_=dp))
 
-    greet(far(px))
     for k in PEERS_Y:
         greet(at(y_=y_peer(k)))
     for k in (2, 1, 3):
         greet(near(x_peer(k)))
     greet(sibling)
 
-    @pl.when(zl > 0)
-    def _():
-        greet(at(z_=zl - 1))
-
-    @pl.when(zl < NZ - 1)
-    def _():
-        greet(at(z_=zl + 1))
+    up_half = jnp.where(zl < NZ - 1, half, other)
+    dn_half = jnp.where(zl > 0, half, other)
+    up = at(dp_=up_half * NX + px, z_=lax.rem(zl + 1, NZ))
+    dn = at(dp_=dn_half * NX + px, z_=lax.rem(zl + NZ - 1, NZ))
+    greet(up)
+    greet(dn)
 
     for j in range(2 * NZ):
         pltpu.make_async_copy(weight_hbm.at[:, pl.ds(j * width, width)], weight.at[j], w_sem).start()
@@ -140,8 +134,7 @@
 
     pick(zl)
 
-    ends = jnp.where(zl > 0, 1, 0) + jnp.where(zl < NZ - 1, 1, 0)
-    pl.semaphore_wait(barrier, 12 + ends + jnp.where(far_source, 1, 0))
+    pl.semaphore_wait(barrier, 13 + jnp.where(far_source, 1, 0))
 
     for k in PEERS_Y:
         to = y_peer(k)
@@ -196,8 +189,26 @@
     def part_of(where, h):
         return scaled.at[where, pl.ds(pl.multiple_of(h * part_rows, part_rows), part_rows)]
 
-    def start_cross(h):
-        remote(part_of(dp, h), part_of(dp, h), cross_s.at[h], cross_r.at[h], far(px)).start()
+    def hop_to(q):
+        return up if q < PARTS // 2 else dn
+
+    def hop_first():
+        for q in (0, 2, 1, 3):
+            remote(part_of(dp, q), hop.at[0, q], hop_s.at[0, q], hop_r.at[0, q], hop_to(q)).start()
+
+    def hop_on(d):
+        for q in (0, 2, 1, 3):
+            drain(hop.at[d - 1, q], hop_r.at[d - 1, q])
+            remote(hop.at[d - 1, q], hop.at[d, q], hop_s.at[d, q], hop_r.at[d, q], hop_to(q)).start()
+
+    def hop_last():
+        d = NZ - 1
+        for q in (0, 2, 1, 3):
+            there = 1 - (up_half if q < PARTS // 2 else dn_half)
+            drain(hop.at[d - 1, q], hop_r.at[d - 1, q])
+            remote(
+                hop.at[d - 1, q], part_of(there * NX + px, q), hop_s.at[d, q], hop_r.at[d, q], hop_to(q)
+            ).start()
 
     far_step = 2 + jnp.abs(zl - jnp.where(half == 0, NZ // 2, NZ // 2 - 1))
 
@@ -232,9 +243,9 @@
             pick(above)
             send_picked(above)
 
-        @pl.when(t >= FIRST)
-        def _():
-            start_cross(t - FIRST)
+        @pl.when(t >= 2)
+        def _():
+            hop_on(t - 1)
 
         @pl.when(t == far_step)
         def _():
@@ -242,7 +253,7 @@
 
         return carry
 
-    lax.fori_loop(1, FIRST, pass_tokens, 0)
+    lax.fori_loop(1, 2, pass_tokens, 0)
 
     drain(gate_in.at[0:nslots - CAP], gate_r)
     gate_col = gate_in[...].astype(F32)[:, 0:1]
@@ -251,9 +262,9 @@
         x = x_peer(k)
         remote(scaled.at[dp], scaled.at[dp], sc_s.at[x], sc_r.at[px], near(x)).start()
 
-    lax.fori_loop(FIRST, NZ, pass_tokens, 0)
-    for h in range(NZ - FIRST, PARTS):
-        start_cross(h)
+    hop_first()
+    lax.fori_loop(2, NZ, pass_tokens, 0)
+    hop_last()
 
     drain(weight, w_sem)
     raw[...] = jnp.zeros_like(raw)
@@ -301,23 +312,21 @@
         return carry
 
     lax.fori_loop(0, NX, take_far, 0)
-    lax.fori_loop(0, 6, take_slots, 0)
+    lax.fori_loop(0, 4, take_slots, 0)
 
     twin = other * NX + px
 
-    def pass_part(h):
-        part = scaled.at[twin, pl.ds(2 * h * part_rows, 2 * part_rows)]
-        for i in range(2):
-            drain(part_of(twin, 2 * h + i), cross_r.at[2 * h + i])
+    def pass_part(q):
+        part = part_of(twin, q)
+        drain(part, hop_r.at[NZ - 1, q])
         for k in (2, 1, 3):
             x = x_peer(k)
             remote(part, part, fsc_s.at[x], fsc_r.at[px], near(x)).start()
 
-    pass_part(0)
-    take_slots(6, 0)
-    pass_part(1)
-    take_slots(7, 0)
-    pass_part(2)
+    for q in (0, 2, 1, 3):
+        pass_part(q)
+
+    lax.fori_loop(4, NZ, take_slots, 0)
     last = nearest(NZ - 1)
     drain(slots.at[last, 1 - core], sib_r.at[last])
     add_raw(last, 1 - core)
@@ -352,8 +361,6 @@
 
     lax.fori_loop(1, NX, near_add, 0)
 
-    pass_part(3)
-
     def far_arrive(q, carry):
         src = other * NX + q
         drain(rows.at[src, core, pl.ds(0, nslots - CAP)], fpick_r.at[q])
@@ -421,8 +428,13 @@
         return carry
 
     lax.fori_loop(0, NX, sent_parts, 0)
-    for h in range(PARTS):
-        drain(part_of(dp, h), cross_s.at[h])
+
+    def sent_hops(d, carry):
+        for q in range(PARTS):
+            drain(hop.at[0, q], hop_s.at[d, q])
+        return carry
+
+    lax.fori_loop(0, NZ, sent_hops, 0)
 
 
 def hand_over(hidden_in, wgrad_in, hidden_out, wgrad_out):
@@ -457,6 +469,7 @@
             pltpu.VMEM((nslots, units), F32),
             pltpu.VMEM((nslots, units), F32),
             pltpu.VMEM((2 * NX, nslots, units), BF16),
+            pltpu.VMEM((NZ - 1, PARTS, nslots // PARTS, units), BF16),
             pltpu.VMEM((NX, tokens + 16, width), BF16),
             pltpu.VMEM((NX, nslots, width), BF16),
             pltpu.VMEM((2 * NX, 2, nslots, width), BF16),
@@ -471,7 +484,7 @@
             dma((NX,)), dma((NX,)),
             dma((NX,)), dma((NX,)),
             dma((NX,)), dma((NX,)),
-            dma((PARTS,)), dma((PARTS,)),
+            dma((NZ, PARTS)), dma((NZ, PARTS)),
             dma((NX,)), dma((NX,)), dma((NX,)), dma((NX,)),
         ],
         compiler_params=pltpu.CompilerParams(

time: 102 us -> 96.9 us (0.950)
  the two profiles are of different devices: /device:TPU:15 before, /device:TPU:7 now
where the time goes in v3:
time: 96.9 us; the launch traced here: 95 us
  Pallas kernels  94.3 us (97%)
    pallas_call x1, Pallas kernels, per_device(): pl.pallas_call(kernel, out_shape=(jax.ShapeDtypeStruct((2, nslots, units)...  92 us
    pallas_call x1, Pallas kernels, per_device(): pl.pallas_call(hand_over, out_shape=(jax.ShapeDtypeStruct(hidden_grad.sha...  2.38 us

profile of v3, /device:TPU:7, one launch (start us, length us, event | category | flops | bytes accessed | tf_op | source)
XLA Modules:
  0.0 95.0 jit_solution(14525358320569847795)
XLA Ops:
  0.6 92.0 %moe_backward.1 = (bf16[2,256,512]{2,1,0:T(8,128)(2,1)}, bf16[768,512]{1,0:T(8,128)(2,1)}) custom-call(bf16[64,384]{1,0:T(8,128)(2,1)} %grad_ref.1, s32[2,64]{1,0:T(2,128)} %bitcast.8, bf16[2,64]{1,0:T(2,128)(2,1)} %bitcast.9, bf16[2,256,512]{2,1,0:T(8,128)(2,1)} %bitcast.7, bf16[512,6144]{1,0:T(8,128)(2,1)} %bitcast.6), custom_call_target="tpu_custom_call" | custom-call | tf_op jit(solution)/shard_map/moe_backward/pallas_call | solution.py:450
  92.6 2.4 %hand_over.1 = (bf16[2,256,512]{2,1,0:T(8,128)(2,1)}, bf16[768,512]{1,0:T(8,128)(2,1)}) custom-call(bf16[2,256,512]{2,1,0:T(8,128)(2,1)} %get-tuple-element.6.hidden_in, bf16[768,512]{1,0:T(8,128)(2,1)} %get-tuple-element.7.wgrad_in), custom_call_target="tpu_custom_call" | custom-call | tf_op jit(solution)/shard_map/hand_over/pallas_call | solution.py:495

commit v4 on v3

--- a/solution.py
+++ b/solution.py
@@ -312,7 +312,7 @@
         return carry
 
     lax.fori_loop(0, NX, take_far, 0)
-    lax.fori_loop(0, 4, take_slots, 0)
+    lax.fori_loop(0, 6, take_slots, 0)
 
     twin = other * NX + px
 
@@ -326,20 +326,10 @@
     for q in (0, 2, 1, 3):
         pass_part(q)
 
-    lax.fori_loop(4, NZ, take_slots, 0)
+    lax.fori_loop(6, NZ, take_slots, 0)
     last = nearest(NZ - 1)
     drain(slots.at[last, 1 - core], sib_r.at[last])
     add_raw(last, 1 - core)
-    gated = gate_in[...].astype(F32)[:, 0:1] * raw[...]
-    hidden_ref[0] = (gated * fac_gate[...]).astype(BF16)
-    hidden_ref[1] = (gated * fac_up[...]).astype(BF16)
-
-    def add_total(c, left, right):
-        total[c] += lax.dot_general(left, right, contract_rows, preferred_element_type=F32)
-
-    for c in range(2):
-        add_total(c, slots[dp, c], scaled[dp])
-
     def near_arrive(k, carry):
         x = x_peer(k)
         src = half * NX + x
@@ -349,6 +339,16 @@
         return carry
 
     lax.fori_loop(1, NX, near_arrive, 0)
+
+    gated = gate_in[...].astype(F32)[:, 0:1] * raw[...]
+    hidden_ref[0] = (gated * fac_gate[...]).astype(BF16)
+    hidden_ref[1] = (gated * fac_up[...]).astype(BF16)
+
+    def add_total(c, left, right):
+        total[c] += lax.dot_general(left, right, contract_rows, preferred_element_type=F32)
+
+    for c in range(2):
+        add_total(c, slots[dp, c], scaled[dp])
 
     def near_add(k, carry):
         x = x_peer(k)

time: 96.9 us -> 95.9 us (0.990); the launches traced: 95 us -> 95 us
  no operation moved by 1% of the time
where the time goes in v4:
time: 95.9 us; the launch traced here: 95 us
  Pallas kernels  94.3 us (98%)
    pallas_call x1, Pallas kernels, per_device(): pl.pallas_call(kernel, out_shape=(jax.ShapeDtypeStruct((2, nslots, units)...  92 us
    pallas_call x1, Pallas kernels, per_device(): pl.pallas_call(hand_over, out_shape=(jax.ShapeDtypeStruct(hidden_grad.sha...  2.38 us

profile of v4, /device:TPU:7, one launch (start us, length us, event | category | flops | bytes accessed | tf_op | source)
XLA Modules:
  0.0 95.0 jit_solution(10495443373486579137)
XLA Ops:
  0.6 92.0 %moe_backward.1 = (bf16[2,256,512]{2,1,0:T(8,128)(2,1)}, bf16[768,512]{1,0:T(8,128)(2,1)}) custom-call(bf16[64,384]{1,0:T(8,128)(2,1)} %grad_ref.1, s32[2,64]{1,0:T(2,128)} %bitcast.8, bf16[2,64]{1,0:T(2,128)(2,1)} %bitcast.9, bf16[2,256,512]{2,1,0:T(8,128)(2,1)} %bitcast.7, bf16[512,6144]{1,0:T(8,128)(2,1)} %bitcast.6), custom_call_target="tpu_custom_call" | custom-call | tf_op jit(solution)/shard_map/moe_backward/pallas_call | solution.py:450
  92.6 2.4 %hand_over.1 = (bf16[2,256,512]{2,1,0:T(8,128)(2,1)}, bf16[768,512]{1,0:T(8,128)(2,1)}) custom-call(bf16[2,256,512]{2,1,0:T(8,128)(2,1)} %get-tuple-element.6.hidden_in, bf16[768,512]{1,0:T(8,128)(2,1)} %get-tuple-element.7.wgrad_in), custom_call_target="tpu_custom_call" | custom-call | tf_op jit(solution)/shard_map/hand_over/pallas_call | solution.py:495
